TPU v7x, 32 devices: a whole 2x2x4 slice. The times are simulated.
32 devices in a mesh: groups: 2 (over y), expert: 4 (over z), tensor: 2 (over x), dp: 2 (over core).
Axes of the slice: x: 2, y: 2, z: 4, core: 2. Of those that a mesh axis runs over, the one named last changes fastest.
Arguments:
- tokens: bfloat16 [128, 3072], P(('groups', 'expert', 'tensor', 'dp')), parts along dimension 0, may hold values from -6 to 6
- expert_ids: int32 [128, 4], P(('groups', 'expert', 'tensor', 'dp')), parts along dimension 0, may hold values from 0 to 7, all different within a row; in each aligned block of 4 rows (0 to 3, 4 to 7, ...) at most 3 rows name the same one
- gate_scores: float32 [128, 4], P(('groups', 'expert', 'tensor', 'dp')), parts along dimension 0, may hold values from 0.2 to 1
- gate_weight: bfloat16 [8, 3072, 6144], P('expert', 'dp', 'tensor'), may hold values from -0.109375 to 0.109375
- up_weight: bfloat16 [8, 3072, 6144], P('expert', 'dp', 'tensor'), may hold values from -0.109375 to 0.109375
- down_weight: bfloat16 [8, 6144, 3072], P('expert', 'tensor', 'dp'), may hold values from -0.078125 to 0.078125
Outputs:
- mixed: bfloat16 [128, 3072], P(('groups', 'expert', 'tensor', 'dp')), parts along dimension 0
There are 2 independent parts, one for each index of `groups`. A program takes and returns all parts, laid end to end along the dimension named above; an argument that names none is the same for every part. Nothing has to cross between parts.
Inputs may be any that keep to these rules, and one draw needn't show every extreme that they name: `expert_ids`: each token names 4 different experts. Among the tokens of one device no expert is named by more than 3 tokens, and that bound is reached in every draw.
All inputs are finite; a program needn't handle non-finite values.
Results may differ from a plain program's by a relative error of at most 0.0058.
Values may be sent and summed in bfloat16 or wider, within the bound.
A program may use at most 128 MiB of HBM per device.

v0:
```python
import jax
import jax.numpy as jnp
from jax import lax
from jax.sharding import PartitionSpec as P

EXPERTS = 8
TOP = 4
CAP = 3


def route_tables(expert_ids, gate_scores, owners, local_count, sub_count):
    tok_count = expert_ids.shape[0]
    flat_ids = expert_ids.reshape(-1)
    onehot = (flat_ids[:, None] == jnp.arange(EXPERTS, dtype=jnp.int32)[None, :]).astype(jnp.int32)
    earlier = jnp.cumsum(onehot, axis=0) - onehot
    position = jnp.sum(earlier * onehot, axis=1)
    shares = gate_scores / jnp.sum(gate_scores, axis=1, keepdims=True)
    owner_ids = jnp.arange(owners, dtype=jnp.int32)[:, None, None]
    queue_pos = jnp.arange(CAP, dtype=jnp.int32)[None, :, None]
    local_ids = jnp.arange(local_count, dtype=jnp.int32)[None, None, :]
    target = (owner_ids * local_count + local_ids) // sub_count
    matches = (flat_ids[None, None, None, :] == target[..., None]) & (
        position[None, None, None, :] == queue_pos[..., None]
    )
    matches = matches.reshape(owners * CAP * local_count, tok_count, TOP).astype(jnp.float32)
    picker = jnp.sum(matches, axis=2)
    combine = jnp.sum(matches * shares[None, :, :], axis=2)
    return (picker, combine)


def local(tokens, expert_ids, gate_scores, gate_weight, up_weight, down_weight):
    owners = lax.axis_size("expert")
    dp_lanes = lax.axis_size("dp")
    local_count = gate_weight.shape[0]
    sub_count = owners * local_count // EXPERTS
    model_width = tokens.shape[1]
    half_width = model_width // dp_lanes
    picker, combine = route_tables(expert_ids, gate_scores, owners, local_count, sub_count)
    outgoing = jnp.dot(
        picker.astype(jnp.bfloat16), tokens, preferred_element_type=jnp.float32
    ).astype(jnp.bfloat16)
    outgoing = outgoing.reshape(owners, CAP, local_count, model_width)
    arrived = lax.all_to_all(
        lax.all_to_all(outgoing, "expert", split_axis=0, concat_axis=0, tiled=True),
        "dp",
        split_axis=3,
        concat_axis=1,
        tiled=True,
    )
    own_rows = owners * dp_lanes * CAP
    inputs = arrived.reshape(own_rows, local_count, half_width)
    segment = lax.all_gather(inputs, "tensor", axis=0, tiled=True)
    gate_part = jnp.einsum("rld,ldf->rlf", segment, gate_weight, preferred_element_type=jnp.float32)
    up_part = jnp.einsum("rld,ldf->rlf", segment, up_weight, preferred_element_type=jnp.float32)
    partial_value = jnp.stack([gate_part, up_part], axis=2)
    summed = lax.psum(partial_value, "dp")
    hidden = (jax.nn.silu(summed[:, :, 0]) * summed[:, :, 1]).astype(jnp.bfloat16)
    result = lax.psum_scatter(
        jnp.einsum("rlf,lfd->rld", hidden, down_weight, preferred_element_type=jnp.float32),
        "tensor",
        scatter_dimension=0,
        tiled=True,
    )
    slot_out = result.astype(jnp.bfloat16).reshape(owners, dp_lanes * CAP, local_count, half_width)
    returned_rows = lax.all_to_all(
        lax.all_to_all(slot_out, "expert", split_axis=0, concat_axis=0, tiled=True),
        "dp",
        split_axis=1,
        concat_axis=3,
        tiled=True,
    )
    returned_rows = returned_rows.reshape(owners * CAP * local_count, model_width)
    mixed = jnp.dot(
        combine.T,
        returned_rows.astype(jnp.float32),
        precision=lax.Precision.HIGHEST,
        preferred_element_type=jnp.float32,
    )
    return mixed.astype(jnp.bfloat16)


def solution(mesh):
    return jax.shard_map(
        local,
        mesh=mesh,
        in_specs=(
            P(("groups", "expert", "tensor", "dp"), None),
            P(("groups", "expert", "tensor", "dp"), None),
            P(("groups", "expert", "tensor", "dp"), None),
            P("expert", "dp", "tensor"),
            P("expert", "dp", "tensor"),
            P("expert", "tensor", "dp"),
        ),
        out_specs=P(("groups", "expert", "tensor", "dp"), None),
        check_vma=False,
    )
```

profile of v0, /device:TPU:0, one launch (start us, length us, event | category | flops | bytes accessed | tf_op | source)
XLA Modules:
  0.0 164.7 jit_solution(6730703919217294338)
XLA Ops:
  6.5 0.0 copy-start
  6.5 0.0 all-reduce.2.cloned.1.call-start
  6.5 0.8 eq.51
  7.3 0.1 iota_add_fusion
  7.4 0.1 fusion.4
  7.5 0.1 broadcast_compare_fusion
  7.5 0.8 reduce_sum.37
  8.3 0.8 broadcast_divide_fusion
  9.1 0.2 select_reduce_fusion.1
  9.3 0.1 and.29
  9.4 0.1 convert_reduce_fusion
  9.6 0.0 copy-done
  9.6 0.2 convolution_convert_fusion
  9.7 0.1 reshape.95
  9.8 12.8 %all_to_all.40 = bf16[4,3,2,3072]{3,2,1,0:T(2,128)(2,1)S(1)} all-to-all(bf16[4,3,2,3072]{3,2,1,0:T(2,128)(2,1)S(1)} %reshape.95), channel_id=1, replica_groups=mesh['groups'=2,'expert'=4,'tensor'=2,'dp'=2] {'expert'}, dimensions={0} | all-to-all | bytes 294912 | tf_op jit(solution)/shard_map/all_to_all | solution.py:44
  22.6 8.0 %copy.23 = bf16[4,3,2,3072]{0,2,1,3:T(2,128)(2,1)} copy(bf16[4,3,2,3072]{3,2,1,0:T(2,128)(2,1)S(1)} %all_to_all.40) | data formatting | bytes 294912 | tf_op jit(solution)/shard_map/all_to_all | solution.py:44
  30.6 10.9 %reshape.99 = bf16[2,2,18432]{2,1,0:T(2,128)(2,1)S(1)} reshape(bf16[3072,3,2,4]{3,2,1,0:T(2,128)(2,1)} %bitcast.45) | data formatting | bytes 294912
  41.5 3.8 %all_to_all.41 = bf16[2,2,18432]{2,1,0:T(2,128)(2,1)S(1)} all-to-all(bf16[2,2,18432]{2,1,0:T(2,128)(2,1)S(1)} %reshape.99), channel_id=1, replica_groups=mesh['groups'=2,'expert'=4,'tensor'=2,'dp'=2] {'dp'}, dimensions={0} | all-to-all | bytes 294912 | tf_op jit(solution)/shard_map/all_to_all | solution.py:43
  45.3 11.5 %reshape.100 = bf16[3072,3,2,4]{3,2,1,0:T(2,128)(2,1)} reshape(bf16[2,2,18432]{2,1,0:T(2,128)(2,1)S(1)} %all_to_all.41) | data formatting | bytes 294912
  56.8 10.9 %copy.25 = bf16[4,2,3,2,1536]{4,3,2,1,0:T(2,128)(2,1)S(1)} copy(bf16[4,2,3,2,1536]{0,3,2,4,1:T(2,128)(2,1)} %bitcast.46) | data formatting | bytes 294912 | tf_op jit(solution)/shard_map/all_to_all | solution.py:43
  67.7 6.6 %all_gather.3 = bf16[48,2,1536]{2,0,1:T(8,128)(2,1)S(1)} all-gather(bf16[24,2,1536]{2,0,1:T(8,128)(2,1)S(1)} %copy.26), channel_id=1, replica_groups=mesh['groups'=2,'expert'=4,'tensor'=2,'dp'=2] {'tensor'}, dimensions={0}, use_global_device_ids=true | all-gather | bytes 442368 | tf_op jit(solution)/shard_map/all_gather | solution.py:52
  74.3 8.1 %convolution_bitcast_fusion = f32[48,2,1,3072]{3,0,1,2:T(8,128)S(1)} fusion(bf16[48,2,1536]{2,0,1:T(8,128)(2,1)S(1)} %all_gather.3, bf16[2,1536,3072]{2,1,0:T(8,128)(2,1)} %param.10), kind=kOutput, calls=%fused_computation | convolution fusion | flops 905969664 | bytes 20348928 | tf_op jit(solution)/shard_map/rld,ldf->rlf/dot_general | solution.py:54
  82.5 8.2 %convolution_bitcast_fusion.1 = f32[48,2,1,3072]{3,0,1,2:T(8,128)S(1)} fusion(bf16[48,2,1536]{2,0,1:T(8,128)(2,1)S(1)} %all_gather.3, bf16[2,1536,3072]{2,1,0:T(8,128)(2,1)} %param.9), kind=kOutput, calls=%fused_computation.1 | convolution fusion | flops 905969664 | bytes 20348928 | tf_op jit(solution)/shard_map/rld,ldf->rlf/dot_general | solution.py:53
  90.6 1.6 pad_maximum_fusion
  92.2 0.0 all-reduce.2.cloned.1.call-update
  92.3 0.2 reduce-scatter.2.cloned.1.call-start
  92.5 20.4 %all-reduce.2.cloned.1.call-done = f32[48,2,2,3072]{3,0,1,2:T(8,128)} async-done(((f32[48,2,2,3072]{3,0,1,2:T(8,128)}), f32[48,2,2,3072]{3,0,1,2:T(8,128)}) %all-reduce.2.cloned.1.call-update) | async-done | bytes 2359312 | tf_op jit(solution)/shard_map/psum | solution.py:56
  112.9 0.0 copy-start.1
  112.9 11.2 %convolution_bitcast_fusion.2 = f32[48,2,1536]{2,0,1:T(8,128)} fusion(bf16[2,3072,1536]{2,1,0:T(8,128)(2,1)} %param.11, f32[48,2,2,3072]{3,0,1,2:T(8,128)} %all-reduce.2.cloned.1.call-done), kind=kOutput, calls=%fused_computation.4 | convolution fusion | flops 907739136 | bytes 21823488 | tf_op jit(solution)/shard_map/rlf,lfd->rld/dot_general | solution.py:59
  124.1 0.0 reduce-scatter.2.cloned.1.call-update
  124.1 16.6 %reduce-scatter.2.cloned.1.call-done = f32[24,2,1536]{2,0,1:T(8,128)} async-done(((f32[48,2,1536]{2,0,1:T(8,128)}), f32[24,2,1536]{2,0,1:T(8,128)}) %reduce-scatter.2.cloned.1.call-update) | async-done | bytes 294928 | tf_op jit(solution)/shard_map/reduce_scatter | solution.py:58
  140.7 1.0 convert_element_type.27
  141.7 0.1 copy.27
  141.8 11.1 %all_to_all.42 = bf16[4,6,2,1536]{3,2,1,0:T(2,128)(2,1)S(1)} all-to-all(bf16[4,6,2,1536]{3,2,1,0:T(2,128)(2,1)S(1)} %bitcast.49), channel_id=1, replica_groups=mesh['groups'=2,'expert'=4,'tensor'=2,'dp'=2] {'expert'}, dimensions={0} | all-to-all | bytes 294912 | tf_op jit(solution)/shard_map/all_to_all | solution.py:66
  152.9 0.1 copy.28
  153.0 3.8 %all_to_all.43 = bf16[4,6,2,1536]{3,2,0,1:T(2,128)(2,1)S(1)} all-to-all(bf16[4,6,2,1536]{3,2,0,1:T(2,128)(2,1)S(1)} %copy.28), channel_id=1, replica_groups=mesh['groups'=2,'expert'=4,'tensor'=2,'dp'=2] {'dp'}, dimensions={1} | all-to-all | bytes 294912 | tf_op jit(solution)/shard_map/all_to_all | solution.py:65
  156.9 0.1 copy.30
  157.0 0.9 convolution_convert_fusion.1
  157.9 0.0 copy-done.1
  (6 shorter events, 0.1 us)
Async XLA Ops:
  6.5 3.0 %copy-start = (bf16[4,3072]{1,0:T(4,128)(2,1)S(1)}, bf16[4,3072]{1,0:T(4,128)(2,1)}, u32[]{:S(2)}) copy-start(bf16[4,3072]{1,0:T(4,128)(2,1)} %param.6) | copy-start | bytes 73732
  6.5 106.4 %all-reduce.2.cloned.1.call-start = ((), (), s32[]{:S(2)}) async-start(), calls=%async_computation.5 | async-start | bytes 4718592 | tf_op jit(solution)/shard_map/psum | solution.py:56
  92.3 48.5 %reduce-scatter.2.cloned.1.call-start = ((), (), s32[]{:S(2)}) async-start(), calls=%async_computation.6 | async-start | bytes 884736 | tf_op jit(solution)/shard_map/reduce_scatter | solution.py:58
  112.9 45.0 %copy-start.1 = (bf16[4,3072]{1,0:T(4,128)(2,1)S(1)}, bf16[4,3072]{1,0:T(4,128)(2,1)}, u32[]{:S(2)}) copy-start(bf16[4,3072]{1,0:T(4,128)(2,1)} %param.6) | copy-start | bytes 73732
Sparse Core Ops, SparseCore 0:
  92.4 20.4 all-reduce.1
  124.3 16.4 reduce-scatter.1
where the time goes:
time: 165 us
  local copies, waits for them, and re-layouts  42.5 us (26%)
  blocking collectives  38.1 us (23%)
  waiting for transfers between devices  37 us (22%)
  matrix products  28.5 us (17%)
  between operations  13.5 us (8%)
  other arithmetic  4.74 us (3%)
    unnamed x7, local copies, waits for them, and re-layouts  22.4 us
    psum x1, waiting for transfers between devices, local(): summed = lax.psum(partial_value, 'dp')  20.4 us
    reduce_scatter x1, waiting for transfers between devices, local(): lax.psum_scatter(jnp.einsum('rlf,lfd->rld', hidden, down_weight, preferre...  16.6 us
    all_to_all x1, blocking collectives, local(): lax.all_to_all(outgoing, 'expert', split_axis=0, concat_axis=0, tiled=True)  12.8 us
    dot_general x1, matrix products, local(): jnp.einsum('rlf,lfd->rld', hidden, down_weight, preferred_element_type=jn...  11.2 us
    all_to_all x1, blocking collectives, local(): lax.all_to_all(slot_out, 'expert', split_axis=0, concat_axis=0, tiled=True)  11.1 us
    all_to_all x1, local copies, waits for them, and re-layouts, local(): lax.all_to_all(lax.all_to_all(outgoing, 'expert', split_axis=0, concat_ax...  10.9 us
    dot_general x1, matrix products, local(): jnp.einsum('rld,ldf->rlf', segment, gate_weight, preferred_element_type=j...  8.16 us
  transfers between devices with their start and end apart: 2, of which 2 were waited for; matrix products, arithmetic and copies ran while one was open for 0% of the time, Pallas kernels for 0%

commit v1 on v0

--- a/solution.py
+++ b/solution.py
@@ -1,11 +1,220 @@
+import functools
+
 import jax
 import jax.numpy as jnp
 from jax import lax
+from jax.experimental import pallas as pl
+from jax.experimental.pallas import tpu as pltpu
 from jax.sharding import PartitionSpec as P
 
 EXPERTS = 8
 TOP = 4
 CAP = 3
+LANES = 128
+MESH = pl.DeviceIdType.MESH
+
+
+def kernel(
+    sizes, tokens, ids, scores, gate_hbm, up_hbm, down_hbm, out,
+    xsend, xrecv, xrows, gate_v, up_v, down_v, own, psend, precv, hidden, shares_v, ysend, yrecv,
+    gate_sem, up_sem, down_sem, xs_sem, xr_sem, ps_sem, pr_sem, ys_sem, yr_sem,
+):
+    n_e, n_t, n_d, slots, sub, tok, half, ff, fc, oc, ring = sizes
+    nf, no = ff // fc, half // oc
+    steps = slots * nf
+    g, e, t, d = (lax.axis_index(name) for name in ("groups", "expert", "tensor", "dp"))
+    me = (e * n_t + t) * n_d + d
+    peers = []
+    for de in reversed(range(n_e)):
+        for dt in reversed(range(n_t)):
+            for dd in reversed(range(n_d)):
+                if de or dt or dd:
+                    pe, pt, pd = lax.rem(e + de, n_e), lax.rem(t + dt, n_t), lax.rem(d + dd, n_d)
+                    peers.append(((g, pe, pt, pd), (pe * n_t + pt) * n_d + pd, pd))
+    other = (g, e, t, lax.rem(d + 1, n_d))
+
+    def weight_copies(step):
+        s, c = step // nf, step % nf
+        cols = pl.ds(pl.multiple_of(c * fc, fc), fc)
+        return (
+            pltpu.make_async_copy(gate_hbm.at[s, :, cols], gate_v.at[step], gate_sem.at[step]),
+            pltpu.make_async_copy(up_hbm.at[s, :, cols], up_v.at[step], up_sem.at[step]),
+        )
+
+    def down_copies(c):
+        return [
+            pltpu.make_async_copy(
+                down_hbm.at[s, :, c * oc : (c + 1) * oc], down_v.at[c, s], down_sem.at[c, s]
+            )
+            for s in range(slots)
+        ]
+
+    def start_weights(step, _):
+        for copy in weight_copies(step):
+            copy.start()
+        return 0
+
+    lax.fori_loop(0, steps, start_weights, 0)
+    for c in range(no):
+        for copy in down_copies(c):
+            copy.start()
+
+    barrier = pltpu.get_barrier_semaphore()
+    for device, _, _ in peers:
+        pl.semaphore_signal(barrier, inc=1, device_id=device, device_id_type=MESH)
+
+    score = scores[...]
+    share = score / jnp.sum(score, axis=1, keepdims=True)
+    lane = lax.broadcasted_iota(jnp.int32, (tok, LANES), 1)
+    table = jnp.zeros((tok, LANES), jnp.float32)
+    for k in range(TOP):
+        table += jnp.where(lane % (LANES // 2) == ids[:, k : k + 1], share[:, k : k + 1], 0.0)
+    high = table.astype(jnp.bfloat16)
+    low = (table - high.astype(jnp.float32)).astype(jnp.bfloat16)
+    tail = jnp.where(lane < LANES // 2, high.astype(jnp.float32), low.astype(jnp.float32)).astype(jnp.bfloat16)
+    for h in range(n_d):
+        xsend[h, :, :half] = tokens[:, h * half : (h + 1) * half]
+        xsend[h, :, half:] = tail
+    xrecv[me] = xsend[d]
+
+    pl.semaphore_wait(barrier, len(peers))
+
+    def token_copy(device, row, pd, at):
+        return pltpu.make_async_remote_copy(
+            src_ref=xsend.at[pd], dst_ref=xrecv.at[at], send_sem=xs_sem.at[row], recv_sem=xr_sem.at[at],
+            device_id=device, device_id_type=MESH,
+        )
+
+    for device, row, pd in peers:
+        token_copy(device, row, pd, me).start()
+    for device, row, pd in peers:
+        token_copy(device, row, pd, row).wait_recv()
+    count = n_e * n_t * n_d
+    for b in range(0, count, 2):
+        pair = jnp.concatenate([xrecv[b].astype(jnp.float32), xrecv[b + 1].astype(jnp.float32)], axis=0)
+        xrows[b * tok : (b + 2) * tok, :] = pair
+    rows = count * tok
+    lanes = lax.broadcasted_iota(jnp.int32, (rows, LANES), 1) % (LANES // 2)
+    for s in range(slots):
+        mine = lanes == (e * slots + s) // sub
+        shares_v[s] = jnp.broadcast_to(
+            jnp.sum(jnp.where(mine, xrows[:, half:], 0.0), axis=1, keepdims=True), (rows, LANES)
+        )
+    x = xrows[:, :half].astype(jnp.bfloat16)
+
+    def partial_copy(step):
+        slot = lax.rem(step, ring)
+        return pltpu.make_async_remote_copy(
+            src_ref=psend.at[slot], dst_ref=precv.at[step], send_sem=ps_sem.at[slot], recv_sem=pr_sem.at[step],
+            device_id=other, device_id_type=MESH,
+        )
+
+    def project(step):
+        for copy in weight_copies(step):
+            copy.wait()
+        slot = lax.rem(step, ring)
+        for at, weight in enumerate((gate_v, up_v)):
+            part = jnp.dot(x, weight[step], preferred_element_type=jnp.float32)
+            own[slot, at] = part
+            psend[slot, at] = part.astype(jnp.bfloat16)
+        partial_copy(step).start()
+
+    def activate(step):
+        slot = lax.rem(step, ring)
+        partial_copy(step).wait()
+        gate = own[slot, 0] + precv[step, 0].astype(jnp.float32)
+        up = own[slot, 1] + precv[step, 1].astype(jnp.float32)
+        s, c = step // nf, step % nf
+        hidden[s, :, pl.ds(pl.multiple_of(c * fc, fc), fc)] = (gate / (1.0 + jnp.exp(-gate)) * up).astype(
+            jnp.bfloat16
+        )
+
+    project(0)
+
+    def up_step(step, _):
+        project(step)
+        activate(step - 1)
+        return 0
+
+    lax.fori_loop(1, steps, up_step, 0)
+    activate(steps - 1)
+
+    def result_copy(device, row, c, at):
+        return pltpu.make_async_remote_copy(
+            src_ref=ysend.at[c, row], dst_ref=yrecv.at[c, at], send_sem=ys_sem.at[c, row],
+            recv_sem=yr_sem.at[c, at], device_id=device, device_id_type=MESH,
+        )
+
+    for c in range(no):
+        total = jnp.zeros((rows, oc), jnp.float32)
+        copies = down_copies(c)
+        for s in range(slots):
+            copies[s].wait()
+            y = jnp.dot(hidden[s], down_v[c, s], preferred_element_type=jnp.float32)
+            total += shares_v[s][:, :1] * y
+        for b in range(count):
+            ysend[c, b] = total[b * tok : (b + 1) * tok, :].astype(jnp.bfloat16)
+        for device, row, _ in peers:
+            result_copy(device, row, c, me).start()
+        yrecv[c, me] = ysend[c, me]
+    for c in range(no):
+        for device, row, _ in peers:
+            result_copy(device, row, c, row).wait_recv()
+        for h in range(n_d):
+            total = jnp.zeros((tok, oc), jnp.float32)
+            for b in range(h, count, n_d):
+                total += yrecv[c, b].astype(jnp.float32)
+            out[:, h * half + c * oc : h * half + (c + 1) * oc] = total.astype(jnp.bfloat16)
+    for device, row, pd in peers:
+        token_copy(device, row, pd, me).wait_send()
+        for c in range(no):
+            result_copy(device, row, c, me).wait_send()
+
+
+def fused(mesh, tokens, expert_ids, gate_scores, gate_weight, up_weight, down_weight):
+    n_e, n_t, n_d = (mesh.shape[name] for name in ("expert", "tensor", "dp"))
+    tok, width = tokens.shape
+    slots, half, ff = gate_weight.shape
+    sub = n_e * slots // EXPERTS
+    fc, oc, ring = 512, 512, 3
+    count = n_e * n_t * n_d
+    steps, no, rows = slots * ff // fc, half // oc, count * tok
+    sizes = (n_e, n_t, n_d, slots, sub, tok, half, ff, fc, oc, ring)
+    dma, bf16, f32 = pltpu.SemaphoreType.DMA, jnp.bfloat16, jnp.float32
+    vmem, hbm = pl.BlockSpec(memory_space=pltpu.VMEM), pl.BlockSpec(memory_space=pl.ANY)
+    return pl.pallas_call(
+        functools.partial(kernel, sizes),
+        out_shape=jax.ShapeDtypeStruct((tok, width), bf16),
+        in_specs=[vmem] * 3 + [hbm] * 3,
+        out_specs=vmem,
+        scratch_shapes=[
+            pltpu.VMEM((n_d, tok, half + LANES), bf16),
+            pltpu.VMEM((count, tok, half + LANES), bf16),
+            pltpu.VMEM((rows, half + LANES), f32),
+            pltpu.VMEM((steps, half, fc), bf16),
+            pltpu.VMEM((steps, half, fc), bf16),
+            pltpu.VMEM((no, slots, ff, oc), bf16),
+            pltpu.VMEM((ring, 2, rows, fc), f32),
+            pltpu.VMEM((ring, 2, rows, fc), bf16),
+            pltpu.VMEM((steps, 2, rows, fc), bf16),
+            pltpu.VMEM((slots, rows, ff), bf16),
+            pltpu.VMEM((slots, rows, LANES), f32),
+            pltpu.VMEM((no, count, tok, oc), bf16),
+            pltpu.VMEM((no, count, tok, oc), bf16),
+            dma((steps,)),
+            dma((steps,)),
+            dma((no, slots)),
+            dma((count,)),
+            dma((count,)),
+            dma((ring,)),
+            dma((steps,)),
+            dma((no, count)),
+            dma((no, count)),
+        ],
+        compiler_params=pltpu.CompilerParams(
+            collective_id=0, has_side_effects=True, vmem_limit_bytes=63 * 2**20
+        ),
+    )(tokens, expert_ids, gate_scores, gate_weight, up_weight, down_weight)
 
 
 def route_tables(expert_ids, gate_scores, owners, local_count, sub_count):
@@ -28,7 +237,7 @@
     return (picker, combine)
 
 
-def local(tokens, expert_ids, gate_scores, gate_weight, up_weight, down_weight):
+def routed(tokens, expert_ids, gate_scores, gate_weight, up_weight, down_weight):
     owners = lax.axis_size("expert")
     dp_lanes = lax.axis_size("dp")
     local_count = gate_weight.shape[0]
@@ -80,8 +289,9 @@
 
 
 def solution(mesh):
+    group = mesh.shape["expert"] * mesh.shape["tensor"] * mesh.shape["dp"]
     return jax.shard_map(
-        local,
+        functools.partial(fused, mesh) if group <= 16 and mesh.shape["dp"] == 2 else routed,
         mesh=mesh,
         in_specs=(
             P(("groups", "expert", "tensor", "dp"), None),

time: 165 us -> 37 us (0.22)
  local copies, waits for them, and re-layouts: 42.5 us -> 1.36 us
  blocking collectives: 38.1 us -> 0 us
  waiting for transfers between devices: 37 us -> 0 us
  Pallas kernels: 0 us -> 35.4 us
  matrix products: 28.5 us -> 0 us
  between operations: 13.5 us -> 0.01 us
  other arithmetic: 4.74 us -> 0 us
    pallas_call x0 -> x1, Pallas kernels: none -> 35.4 us  [fused(): pl.pallas_call(functools.partial(kernel, sizes), out_shape=jax.ShapeDtype...]
    all_to_all x4 -> x0, blocking collectives: 31.5 us -> none  [the longest x1 12.8 us: local(): lax.all_to_all(outgoing, 'expert', split_axis=0, concat_axis=0, tiled=True)]
    dot_general x5 -> x0, matrix products: 28.5 us -> none  [the longest x1 11.2 us: local(): jnp.einsum('rlf,lfd->rld', hidden, down_weight, preferred_element_type=jn...]
    unnamed x7 -> x1, local copies, waits for them, and re-layouts: 22.4 us -> 1.36 us
    psum x1 -> x0, waiting for transfers between devices: 20.4 us -> none  [local(): summed = lax.psum(partial_value, 'dp')]
    all_to_all x4 -> x0, local copies, waits for them, and re-layouts: 19.1 us -> none  [the longest x1 10.9 us: local(): lax.all_to_all(lax.all_to_all(outgoing, 'expert', split_axis=0, concat_ax...]
    reduce_scatter x1 -> x0, waiting for transfers between devices: 16.6 us -> none  [local(): lax.psum_scatter(jnp.einsum('rlf,lfd->rld', hidden, down_weight, preferre...]
    all_gather x1 -> x0, blocking collectives: 6.59 us -> none  [local(): segment = lax.all_gather(inputs, 'tensor', axis=0, tiled=True)]
  transfers between devices with their start and end apart: 2 -> 0, of which waited for: 2 -> 0; matrix products, arithmetic and copies ran while one was open for 0% -> 0% of each run, Pallas kernels for 0% -> 0%
where the time goes in v1:
time: 37 us; the launch traced here: 36.8 us
  Pallas kernels  35.4 us (96%)
  local copies, waits for them, and re-layouts  1.36 us (4%)
    pallas_call x1, Pallas kernels, fused(): pl.pallas_call(functools.partial(kernel, sizes), out_shape=jax.ShapeDtype...  35.4 us
    unnamed x1, local copies, waits for them, and re-layouts  1.36 us

profile of v1, /device:TPU:0, one launch (start us, length us, event | category | flops | bytes accessed | tf_op | source)
XLA Modules:
  0.0 36.8 jit_solution(10835324816739752940)
XLA Ops:
  0.0 35.4 %shard_map.64 = bf16[4,3072]{1,0:T(4,128)(2,1)} custom-call(bf16[4,3072]{1,0:T(4,128)(2,1)} %tokens.1, s32[4,4]{1,0:T(4,128)} %ids.1, f32[4,4]{1,0:T(4,128)} %scores.1, bf16[2,1536,3072]{2,1,0:T(8,128)(2,1)} %gate_hbm.1, bf16[2,1536,3072]{2,1,0:T(8,128)(2,1)} %up_hbm.1, bf16[2,3072,1536]{2,1,0:T(8,128)(2,1)} %down_hbm.1), custom_call_target="tpu_custom_call" | custom-call | tf_op jit(solution)/shard_map/pallas_call | solution.py:185
  35.4 1.4 %copy.8 = bf16[4,3072]{1,0:T(4,128)(2,1)} copy(bf16[4,3072]{1,0:T(4,128)(2,1)} %shard_map.64) | data formatting | bytes 49152

commit v2 on v1

--- a/solution.py
+++ b/solution.py
@@ -16,22 +16,22 @@
 
 def kernel(
     sizes, tokens, ids, scores, gate_hbm, up_hbm, down_hbm, out,
-    xsend, xrecv, xrows, gate_v, up_v, down_v, own, psend, precv, hidden, shares_v, ysend, yrecv,
-    gate_sem, up_sem, down_sem, xs_sem, xr_sem, ps_sem, pr_sem, ys_sem, yr_sem,
+    xsend, xother, xrecv, xrows, gate_v, up_v, down_v, own, psend, precv, hidden, shares_v, ysend, yrecv, zsend, zrecv,
+    gate_sem, up_sem, down_sem, xo_sem, xs_sem, xr_sem, ps_sem, pr_sem, ys_sem, yr_sem, z_sem,
 ):
     n_e, n_t, n_d, slots, sub, tok, half, ff, fc, oc, ring = sizes
     nf, no = ff // fc, half // oc
     steps = slots * nf
     g, e, t, d = (lax.axis_index(name) for name in ("groups", "expert", "tensor", "dp"))
-    me = (e * n_t + t) * n_d + d
+    me, chips = e * n_t + t, n_e * n_t
     peers = []
     for de in reversed(range(n_e)):
         for dt in reversed(range(n_t)):
-            for dd in reversed(range(n_d)):
-                if de or dt or dd:
-                    pe, pt, pd = lax.rem(e + de, n_e), lax.rem(t + dt, n_t), lax.rem(d + dd, n_d)
-                    peers.append(((g, pe, pt, pd), (pe * n_t + pt) * n_d + pd, pd))
-    other = (g, e, t, lax.rem(d + 1, n_d))
+            if de or dt:
+                pe, pt = lax.rem(e + de, n_e), lax.rem(t + dt, n_t)
+                peers.append(((g, pe, pt, d), pe * n_t + pt))
+    od = lax.rem(d + 1, n_d)
+    other = (g, e, t, od)
 
     def weight_copies(step):
         s, c = step // nf, step % nf
@@ -60,7 +60,7 @@
             copy.start()
 
     barrier = pltpu.get_barrier_semaphore()
-    for device, _, _ in peers:
+    for device in [other] + [device for device, _ in peers]:
         pl.semaphore_signal(barrier, inc=1, device_id=device, device_id_type=MESH)
 
     score = scores[...]
@@ -75,25 +75,33 @@
     for h in range(n_d):
         xsend[h, :, :half] = tokens[:, h * half : (h + 1) * half]
         xsend[h, :, half:] = tail
-    xrecv[me] = xsend[d]
-
-    pl.semaphore_wait(barrier, len(peers))
-
-    def token_copy(device, row, pd, at):
+
+    pl.semaphore_wait(barrier, len(peers) + 1)
+
+    swap = pltpu.make_async_remote_copy(
+        src_ref=xsend.at[od], dst_ref=xother, send_sem=xo_sem.at[0], recv_sem=xo_sem.at[1],
+        device_id=other, device_id_type=MESH,
+    )
+    swap.start()
+    swap.wait()
+    mine, theirs = xsend[d].astype(jnp.float32), xother[...].astype(jnp.float32)
+    both = jnp.concatenate([jnp.where(d == 0, mine, theirs), jnp.where(d == 0, theirs, mine)], axis=0)
+    xrecv[me] = both.astype(jnp.bfloat16)
+
+    def token_copy(device, row, at):
         return pltpu.make_async_remote_copy(
-            src_ref=xsend.at[pd], dst_ref=xrecv.at[at], send_sem=xs_sem.at[row], recv_sem=xr_sem.at[at],
+            src_ref=xrecv.at[me], dst_ref=xrecv.at[at], send_sem=xs_sem.at[row], recv_sem=xr_sem.at[at],
             device_id=device, device_id_type=MESH,
         )
 
-    for device, row, pd in peers:
-        token_copy(device, row, pd, me).start()
-    for device, row, pd in peers:
-        token_copy(device, row, pd, row).wait_recv()
-    count = n_e * n_t * n_d
-    for b in range(0, count, 2):
-        pair = jnp.concatenate([xrecv[b].astype(jnp.float32), xrecv[b + 1].astype(jnp.float32)], axis=0)
-        xrows[b * tok : (b + 2) * tok, :] = pair
-    rows = count * tok
+    for device, row in peers:
+        token_copy(device, row, me).start()
+    for device, row in peers:
+        token_copy(device, row, row).wait_recv()
+    pair = n_d * tok
+    rows = chips * pair
+    for b in range(chips):
+        xrows[b * pair : (b + 1) * pair, :] = xrecv[b].astype(jnp.float32)
     lanes = lax.broadcasted_iota(jnp.int32, (rows, LANES), 1) % (LANES // 2)
     for s in range(slots):
         mine = lanes == (e * slots + s) // sub
@@ -152,21 +160,30 @@
             copies[s].wait()
             y = jnp.dot(hidden[s], down_v[c, s], preferred_element_type=jnp.float32)
             total += shares_v[s][:, :1] * y
-        for b in range(count):
-            ysend[c, b] = total[b * tok : (b + 1) * tok, :].astype(jnp.bfloat16)
-        for device, row, _ in peers:
+        for b in range(chips):
+            ysend[c, b] = total[b * pair : (b + 1) * pair, :].astype(jnp.bfloat16)
+        for device, row in peers:
             result_copy(device, row, c, me).start()
         yrecv[c, me] = ysend[c, me]
     for c in range(no):
-        for device, row, _ in peers:
+        for device, row in peers:
             result_copy(device, row, c, row).wait_recv()
-        for h in range(n_d):
-            total = jnp.zeros((tok, oc), jnp.float32)
-            for b in range(h, count, n_d):
-                total += yrecv[c, b].astype(jnp.float32)
-            out[:, h * half + c * oc : h * half + (c + 1) * oc] = total.astype(jnp.bfloat16)
-    for device, row, pd in peers:
-        token_copy(device, row, pd, me).wait_send()
+        total = jnp.zeros((pair, oc), jnp.float32)
+        for b in range(chips):
+            total += yrecv[c, b].astype(jnp.float32)
+        upper, lower = total[:tok], total[tok:]
+        zsend[:, c * oc : (c + 1) * oc] = jnp.where(d == 0, lower, upper).astype(jnp.bfloat16)
+        columns = pl.ds(pl.multiple_of(d * half + c * oc, LANES), oc)
+        out[:, columns] = jnp.where(d == 0, upper, lower).astype(jnp.bfloat16)
+    swap_back = pltpu.make_async_remote_copy(
+        src_ref=zsend, dst_ref=zrecv, send_sem=z_sem.at[0], recv_sem=z_sem.at[1],
+        device_id=other, device_id_type=MESH,
+    )
+    swap_back.start()
+    swap_back.wait()
+    out[:, pl.ds(pl.multiple_of(od * half, LANES), half)] = zrecv[...]
+    for device, row in peers:
+        token_copy(device, row, me).wait_send()
         for c in range(no):
             result_copy(device, row, c, me).wait_send()
 
@@ -177,8 +194,8 @@
     slots, half, ff = gate_weight.shape
     sub = n_e * slots // EXPERTS
     fc, oc, ring = 512, 512, 3
-    count = n_e * n_t * n_d
-    steps, no, rows = slots * ff // fc, half // oc, count * tok
+    count, pair = n_e * n_t, n_d * tok
+    steps, no, rows = slots * ff // fc, half // oc, count * pair
     sizes = (n_e, n_t, n_d, slots, sub, tok, half, ff, fc, oc, ring)
     dma, bf16, f32 = pltpu.SemaphoreType.DMA, jnp.bfloat16, jnp.float32
     vmem, hbm = pl.BlockSpec(memory_space=pltpu.VMEM), pl.BlockSpec(memory_space=pl.ANY)
@@ -189,7 +206,8 @@
         out_specs=vmem,
         scratch_shapes=[
             pltpu.VMEM((n_d, tok, half + LANES), bf16),
-            pltpu.VMEM((count, tok, half + LANES), bf16),
+            pltpu.VMEM((tok, half + LANES), bf16),
+            pltpu.VMEM((count, pair, half + LANES), bf16),
             pltpu.VMEM((rows, half + LANES), f32),
             pltpu.VMEM((steps, half, fc), bf16),
             pltpu.VMEM((steps, half, fc), bf16),
@@ -199,17 +217,21 @@
             pltpu.VMEM((steps, 2, rows, fc), bf16),
             pltpu.VMEM((slots, rows, ff), bf16),
             pltpu.VMEM((slots, rows, LANES), f32),
-            pltpu.VMEM((no, count, tok, oc), bf16),
-            pltpu.VMEM((no, count, tok, oc), bf16),
+            pltpu.VMEM((no, count, pair, oc), bf16),
+            pltpu.VMEM((no, count, pair, oc), bf16),
+            pltpu.VMEM((tok, half), bf16),
+            pltpu.VMEM((tok, half), bf16),
             dma((steps,)),
             dma((steps,)),
             dma((no, slots)),
+            dma((2,)),
             dma((count,)),
             dma((count,)),
             dma((ring,)),
             dma((steps,)),
             dma((no, count)),
             dma((no, count)),
+            dma((2,)),
         ],
         compiler_params=pltpu.CompilerParams(
             collective_id=0, has_side_effects=True, vmem_limit_bytes=63 * 2**20

time: 37 us -> 38 us (1.027)
  Pallas kernels: 35.4 us -> 36.4 us
    pallas_call x1, Pallas kernels: 35.4 us -> 36.4 us  [fused(): pl.pallas_call(functools.partial(kernel, sizes), out_shape=jax.ShapeDtype...]
where the time goes in v2:
time: 38 us; the launch traced here: 37.8 us
  Pallas kernels  36.4 us (96%)
  local copies, waits for them, and re-layouts  1.36 us (4%)
    pallas_call x1, Pallas kernels, fused(): pl.pallas_call(functools.partial(kernel, sizes), out_shape=jax.ShapeDtype...  36.4 us
    unnamed x1, local copies, waits for them, and re-layouts  1.36 us

profile of v2, /device:TPU:0, one launch (start us, length us, event | category | flops | bytes accessed | tf_op | source)
XLA Modules:
  0.0 37.8 jit_solution(9270123892245574103)
XLA Ops:
  0.0 36.4 %shard_map.64 = bf16[4,3072]{1,0:T(4,128)(2,1)} custom-call(bf16[4,3072]{1,0:T(4,128)(2,1)} %tokens.1, s32[4,4]{1,0:T(4,128)} %ids.1, f32[4,4]{1,0:T(4,128)} %scores.1, bf16[2,1536,3072]{2,1,0:T(8,128)(2,1)} %gate_hbm.1, bf16[2,1536,3072]{2,1,0:T(8,128)(2,1)} %up_hbm.1, bf16[2,3072,1536]{2,1,0:T(8,128)(2,1)} %down_hbm.1), custom_call_target="tpu_custom_call" | custom-call | tf_op jit(solution)/shard_map/pallas_call | solution.py:202
  36.4 1.4 %copy.8 = bf16[4,3072]{1,0:T(4,128)(2,1)} copy(bf16[4,3072]{1,0:T(4,128)(2,1)} %shard_map.64) | data formatting | bytes 49152

commit v3 on v1

--- a/solution.py
+++ b/solution.py
@@ -130,14 +130,17 @@
         )
 
     project(0)
+    project(1)
 
     def up_step(step, _):
         project(step)
-        activate(step - 1)
+        activate(step - 2)
         return 0
 
-    lax.fori_loop(1, steps, up_step, 0)
-    activate(steps - 1)
+    lax.fori_loop(2, steps, up_step, 0)
+    activate(steps - 2)
+    if slots == 1:
+        activate(steps - 1)
 
     def result_copy(device, row, c, at):
         return pltpu.make_async_remote_copy(
@@ -152,6 +155,8 @@
             copies[s].wait()
             y = jnp.dot(hidden[s], down_v[c, s], preferred_element_type=jnp.float32)
             total += shares_v[s][:, :1] * y
+            if c == 0 and s == 0 and slots > 1:
+                activate(steps - 1)
         for b in range(count):
             ysend[c, b] = total[b * tok : (b + 1) * tok, :].astype(jnp.bfloat16)
         for device, row, _ in peers:

time: 37 us -> 34.5 us (0.932)
  Pallas kernels: 35.4 us -> 32.9 us
    pallas_call x1, Pallas kernels: 35.4 us -> 32.9 us  [fused(): pl.pallas_call(functools.partial(kernel, sizes), out_shape=jax.ShapeDtype...]
where the time goes in v3:
time: 34.5 us; the launch traced here: 34.3 us
  Pallas kernels  32.9 us (95%)
  local copies, waits for them, and re-layouts  1.36 us (4%)
    pallas_call x1, Pallas kernels, fused(): pl.pallas_call(functools.partial(kernel, sizes), out_shape=jax.ShapeDtype...  32.9 us
    unnamed x1, local copies, waits for them, and re-layouts  1.36 us

profile of v3, /device:TPU:0, one launch (start us, length us, event | category | flops | bytes accessed | tf_op | source)
XLA Modules:
  0.0 34.3 jit_solution(1689820356789623569)
XLA Ops:
  0.0 32.9 %shard_map.64 = bf16[4,3072]{1,0:T(4,128)(2,1)} custom-call(bf16[4,3072]{1,0:T(4,128)(2,1)} %tokens.1, s32[4,4]{1,0:T(4,128)} %ids.1, f32[4,4]{1,0:T(4,128)} %scores.1, bf16[2,1536,3072]{2,1,0:T(8,128)(2,1)} %gate_hbm.1, bf16[2,1536,3072]{2,1,0:T(8,128)(2,1)} %up_hbm.1, bf16[2,3072,1536]{2,1,0:T(8,128)(2,1)} %down_hbm.1), custom_call_target="tpu_custom_call" | custom-call | tf_op jit(solution)/shard_map/pallas_call | solution.py:190
  32.9 1.4 %copy.8 = bf16[4,3072]{1,0:T(4,128)(2,1)} copy(bf16[4,3072]{1,0:T(4,128)(2,1)} %shard_map.64) | data formatting | bytes 49152
